TPU v7x, 32 devices: a whole 2x2x4 slice. The times are simulated.
32 devices in a mesh: cd: 8 (over z, core), ij: 4 (over y, x).
Axes of the slice: x: 2, y: 2, z: 4, core: 2. Of those that a mesh axis runs over, the one named last changes fastest.
Arguments:
- left_factor: bfloat16 [4096, 4096], P('cd'), may hold values from -6 to 6
- right_factor: bfloat16 [4096, 4, 1024], P(None, None, 'ij'), may hold values from -0.09375 to 0.09375
- amplitudes: float32 [8, 192, 1024], P('ij', 'cd'), may hold values from -0.0390625 to 0.0390625
- heights: int32 [8], P('cd'), may hold values from 256 to 512, as said below
- owner_map: int32 [8, 512, 1], P('cd'), may hold values from 0 to 7; in each aligned block of 512 rows (0 to 511, 512 to 1023, ..., all dimensions but the last counted through in order) at most 96 rows name the same one
- row_site: int32 [8, 512], P('cd'), may hold values from 0 to 23
Outputs:
- residual: float32 [32], P(('ij', 'cd'))
Inputs may be any that keep to these rules, and one draw needn't show every extreme that they name: `heights`: some former has exactly 512 live rows. `owner_map`: within the 512 rows of one former no tile is named more than 96 times, and that bound is reached.
All inputs are finite; a program needn't handle non-finite values.
Results may differ from a plain program's by a relative error of at most 0.0028.
Values may be sent and summed in bfloat16 or wider, within the bound.
A program may use at most 64 MiB of HBM per device.

v0:
```python
import jax
import jax.numpy as jnp
from jax import lax
from jax.sharding import PartitionSpec as P


def contract(amplitudes, sums):
    return jnp.einsum("icd,cbd->ib", amplitudes, sums, precision=lax.Precision.HIGHEST)


def on_device(left_factor, right_factor, amplitudes, heights, owner_map, row_site):
    rows = left_factor.shape[0]
    formers = lax.axis_size("cd")
    capacity = (rows + formers - 1) // formers + rows // (2 * formers)
    bwidth = right_factor.shape[1]
    dpiece = right_factor.shape[2]
    tile = amplitudes.shape[1]
    panel = jnp.dot(
        left_factor,
        right_factor.reshape(right_factor.shape[0], -1),
        preferred_element_type=jnp.float32,
    )
    position = jnp.arange(rows, dtype=jnp.int32)
    live = position < heights[0]
    panel = jnp.where(live[:, None], panel, 0.0).astype(jnp.bfloat16)
    owners = owner_map[0, :, 0]
    hits = (owners[:, None] == jnp.arange(formers, dtype=jnp.int32)[None, :]) & live[:, None]
    places = jnp.cumsum(hits.astype(jnp.int32), axis=0) - 1
    within = jnp.sum(jnp.where(hits, places, 0), axis=1)
    target = jnp.where(live, owners * capacity + within, -1)
    dispatch = jnp.arange(formers * capacity, dtype=jnp.int32)[:, None] == target[None, :]
    outgoing = jnp.dot(
        dispatch.astype(jnp.bfloat16), panel, preferred_element_type=jnp.float32
    ).astype(jnp.bfloat16)
    labels = jnp.dot(dispatch.astype(jnp.float32), row_site[0].astype(jnp.float32)).astype(
        jnp.int32
    )
    outgoing = outgoing.reshape(formers, capacity, bwidth, dpiece)
    labels = labels.reshape(formers, capacity)
    arrived, arrived_labels = (
        lax.all_to_all(outgoing, "cd", split_axis=0, concat_axis=0, tiled=True),
        lax.all_to_all(labels, "cd", split_axis=0, concat_axis=0, tiled=True),
    )
    arrived = arrived.reshape(formers * capacity, bwidth, dpiece)
    picker = (
        jnp.arange(tile, dtype=jnp.int32)[:, None] == arrived_labels.reshape(-1)[None, :]
    ).astype(jnp.bfloat16)
    whole = lax.all_gather(
        jnp.einsum("cr,rbd->cbd", picker, arrived, preferred_element_type=jnp.float32),
        "ij",
        axis=2,
        tiled=True,
    )
    partial_value = contract(amplitudes, whole)
    return lax.psum_scatter(partial_value.reshape(-1), "cd", scatter_dimension=0, tiled=True)


def solution(mesh):
    placed = (
        P("cd", None),
        P(None, None, "ij"),
        P("ij", "cd", None),
        P("cd"),
        P("cd", None, None),
        P("cd", None),
    )
    return jax.shard_map(
        on_device, mesh=mesh, in_specs=placed, out_specs=P(("ij", "cd")), check_vma=False
    )
```

profile of v0, /device:TPU:0, one launch (start us, length us, event | category | flops | bytes accessed | tf_op | source)
XLA Modules:
  0.0 104.7 jit_solution(13899292502363692170)
XLA Ops:
  0.0 0.0 copy-start
  0.7 0.7 fusion.13
  1.4 1.1 %reduce-window.6 = s32[8,4,128]{2,0,1:T(8,128)S(1)} reduce-window(s32[8,4,128]{2,0,1:T(8,128)S(1)} %fusion.13, s32[]{:T(128)} %constant.12.clone.1), window={size=1x1x128 pad=0_0x0_0x127_0}, to_apply=%region_0.1 | reduce-window | flops 520192 | bytes 32772 | tf_op jit(solution)/shard_map/reduce-window
  2.5 0.2 slice_reduce_fusion
  2.8 0.8 fusion.10
  3.6 0.7 add_select_fusion
  4.3 1.1 %fusion.1 = f32[768]{0:T(1024)S(1)} fusion(s32[512]{0:T(512)S(1)} %add_select_fusion, s32[1,512]{1,0:T(1,128)} %param.11), kind=kOutput, calls=%fused_computation.4 | convolution fusion | flops 1180160 | bytes 7168 | tf_op jit(solution)/shard_map/dot_general | solution.py:35
  5.3 0.7 all_to_all.9
  6.0 6.3 %all-to-all-start = ((s32[8,1,96]{2,1,0:T(1,128)}), s32[8,1,96]{2,1,0:T(1,128)S(1)}, u32[]{:S(2)}, u32[]{:S(2)}) async-start(s32[8,1,96]{2,1,0:T(1,128)} %all_to_all.9), calls=%async_computation | async-start | bytes 8192 | tf_op jit(solution)/shard_map/all_to_all | solution.py:42
  12.3 9.4 %copy.12 = bf16[512,8,4,256]{3,1,2,0:T(8,128)(2,1)} copy(bf16[512,8,4,256]{3,2,1,0:T(4,128)(2,1)} %bitcast.30) | data formatting | bytes 16777216
  21.7 10.0 %convolution_convert_fusion = bf16[768,1024]{1,0:T(8,128)(2,1)S(1)} fusion(bf16[512,4096]{1,0:T(8,128)(2,1)} %param.6, bf16[4096,1024]{1,0:T(8,128)(2,1)} %bitcast.31, pred[512]{0:T(512)(128)(4,1)S(1)} %iota_compare_fusion.8, s32[512]{0:T(512)S(1)} %add_select_fusion), kind=kOutput, calls=%fused_computation.1 | convolution fusion | flops 5102501888 | bytes 14158336 | tf_op jit(solution)/shard_map/dot_general | solution.py:32
  31.6 2.4 %reshape.63 = bf16[8,96,4,256]{3,2,1,0:T(4,128)(2,1)} reshape(bf16[768,1024]{1,0:T(8,128)(2,1)S(1)} %convolution_convert_fusion) | data formatting | bytes 3145728 | tf_op jit(solution)/shard_map/reshape | solution.py:38
  34.0 0.0 all-to-all-done
  34.0 5.1 %all-to-all-start.1 = ((bf16[8,96,4,256]{3,2,1,0:T(4,128)(2,1)}), bf16[8,96,4,256]{3,2,1,0:T(4,128)(2,1)S(1)}, u32[]{:S(2)}, u32[]{:S(2)}) async-start(bf16[8,96,4,256]{3,2,1,0:T(4,128)(2,1)} %reshape.63), calls=%async_computation.1 | async-start | bytes 3145728 | tf_op jit(solution)/shard_map/all_to_all | solution.py:41
  39.1 0.5 broadcast.49
  39.6 0.7 reduce.7
  40.3 0.1 eq.62
  40.4 36.6 %all-to-all-done.1 = bf16[8,96,4,256]{3,2,1,0:T(4,128)(2,1)S(1)} async-done(((bf16[8,96,4,256]{3,2,1,0:T(4,128)(2,1)}), bf16[8,96,4,256]{3,2,1,0:T(4,128)(2,1)S(1)}, u32[]{:S(2)}, u32[]{:S(2)}) %all-to-all-start.1) | async-done | bytes 1572896 | tf_op jit(solution)/shard_map/all_to_all | solution.py:41
  77.0 0.3 copy.9
  77.2 0.0 copy-start.1
  77.3 0.3 fusion.7
  77.6 9.5 %all_gather.3 = f32[24,4,1024]{2,0,1:T(8,128)S(1)} all-gather(f32[24,4,256]{2,0,1:T(8,128)S(1)} %fusion.7), channel_id=1, replica_groups=mesh['cd'=8,'ij'=4] {'ij'}, dimensions={2}, use_global_device_ids=true | all-gather | bytes 491520 | tf_op jit(solution)/shard_map/all_gather | solution.py:48
  87.1 0.0 copy-done
  87.1 1.9 %convolution_bitcast_fusion = f32[2,4]{1,0:T(2,128)S(1)} fusion(f32[24,4,1024]{2,0,1:T(8,128)S(1)} %all_gather.3, f32[2,24,1024]{2,1,0:T(8,128)S(1)} %copy-done), kind=kOutput, calls=%fused_computation.5 | convolution fusion | flops 2359296 | bytes 589856 | tf_op jit(solution)/shard_map/icd,cbd->ib/dot_general | solution.py:8
  89.0 0.1 reshape.65
  89.1 0.0 copy-done.1
  89.1 0.7 dynamic-slice
  89.8 13.6 %all-reduce = f32[8]{0:T(128)S(1)} all-reduce(f32[8]{0:T(128)S(1)} %reshape.65), channel_id=2, replica_groups=mesh['cd'=8,'ij'=4] {'cd'}, use_global_device_ids=true, to_apply=%region_3.4.clone | all-reduce | flops 8 | bytes 64
  103.4 1.3 %dynamic-slice.1 = f32[1]{0:T(128)} dynamic-slice(f32[8]{0:T(128)S(1)} %all-reduce, u32[]{:T(128)} %bitcast.13), dynamic_slice_sizes={1} | dynamic-slice | bytes 12
  (5 shorter events, 0.1 us)
Async XLA Ops:
  0.0 87.1 %copy-start = (f32[2,24,1024]{2,1,0:T(8,128)S(1)}, f32[2,24,1024]{2,1,0:T(8,128)}, u32[]{:S(2)}) copy-start(f32[2,24,1024]{2,1,0:T(8,128)} %param.8) | copy-start | bytes 589828
  6.0 28.0 %all-to-all-start = ((s32[8,1,96]{2,1,0:T(1,128)}), s32[8,1,96]{2,1,0:T(1,128)S(1)}, u32[]{:S(2)}, u32[]{:S(2)}) async-start(s32[8,1,96]{2,1,0:T(1,128)} %all_to_all.9), calls=%async_computation | async-start | bytes 8192 | tf_op jit(solution)/shard_map/all_to_all | solution.py:42
  34.0 42.9 %all-to-all-start.1 = ((bf16[8,96,4,256]{3,2,1,0:T(4,128)(2,1)}), bf16[8,96,4,256]{3,2,1,0:T(4,128)(2,1)S(1)}, u32[]{:S(2)}, u32[]{:S(2)}) async-start(bf16[8,96,4,256]{3,2,1,0:T(4,128)(2,1)} %reshape.63), calls=%async_computation.1 | async-start | bytes 3145728 | tf_op jit(solution)/shard_map/all_to_all | solution.py:41
  77.2 11.9 %copy-start.1 = (u32[32]{0:T(128)S(1)}, u32[32]{0:T(128)}, u32[]{:S(2)}) copy-start(u32[32]{0:T(128)} %constant.21) | copy-start | bytes 388
where the time goes:
time: 105 us
  waiting for transfers between devices  36.6 us (35%)
  blocking collectives  23.1 us (22%)
  local copies, waits for them, and re-layouts  15.5 us (15%)
  matrix products  13.3 us (13%)
  starting transfers between devices  11.4 us (11%)
  other arithmetic  3.99 us (4%)
    all_to_all x1, waiting for transfers between devices, on_device(): lax.all_to_all(outgoing, 'cd', split_axis=0, concat_axis=0, tiled=True)  36.6 us
    unnamed x1, blocking collectives  13.6 us
    unnamed x7, local copies, waits for them, and re-layouts  11.3 us
    dot_general x1, matrix products, on_device(): jnp.dot(dispatch.astype(jnp.bfloat16), panel, preferred_element_type=jnp....  9.96 us
    all_gather x1, blocking collectives, on_device(): lax.all_gather(jnp.einsum('cr,rbd->cbd', picker, arrived, preferred_eleme...  9.52 us
    all_to_all x1, starting transfers between devices, on_device(): lax.all_to_all(labels, 'cd', split_axis=0, concat_axis=0, tiled=True)  6.33 us
    all_to_all x1, starting transfers between devices, on_device(): lax.all_to_all(outgoing, 'cd', split_axis=0, concat_axis=0, tiled=True)  5.1 us
    reshape x1, local copies, waits for them, and re-layouts, on_device(): outgoing = outgoing.reshape(formers, capacity, bwidth, dpiece)  2.39 us
  transfers between devices with their start and end apart: 2, of which 1 were waited for; matrix products, arithmetic and copies ran while one was open for 22% of the time, Pallas kernels for 0%

commit v1 on v0

--- a/solution.py
+++ b/solution.py
@@ -1,14 +1,281 @@
+import functools
+
 import jax
 import jax.numpy as jnp
 from jax import lax
+from jax.experimental import pallas as pl
+from jax.experimental.pallas import tpu as pltpu
 from jax.sharding import PartitionSpec as P
+
+LANES = 128
+SIDE = 256
+MESH = pl.DeviceIdType.MESH
+
+
+def ladder_kernel(
+    formers, blocks, nb, depth_chunks,
+    amp_ref, label_ref, left_ref, right_ref, out_ref,
+    left_v, right_v, sorted_v, first_panel, sums, pair_in, joined, tiles_in, amp_in, rows_out, rows_in,
+    left_sem, right_sem, amp_send, amp_recv, pair_send, pair_recv,
+    tile_send, tile_recv, row_send, row_recv,
+):
+    f = lax.axis_index("cd")
+    j = lax.axis_index("ij")
+    chips = formers // 2
+    z = lax.div(f, 2)
+    core = lax.rem(f, 2)
+    devices = formers * blocks
+    me = j * formers + f
+
+    rows, depth = left_v.shape
+    kc = depth // depth_chunks
+    lane_tiles = right_v.shape[0] // (depth * nb)
+    group = nb * lane_tiles
+    per = SIDE // group
+    dpiece = lane_tiles * LANES
+    ni, tile, _ = amp_ref.shape
+
+    def load(k):
+        return (
+            pltpu.make_async_copy(
+                right_ref.at[pl.ds(k * kc * group, kc * group)],
+                right_v.at[pl.ds(k * kc * group, kc * group)],
+                right_sem.at[k],
+            ),
+            pltpu.make_async_copy(
+                left_ref.at[:, pl.ds(k * kc, kc)],
+                left_v.at[:, pl.ds(k * kc, kc)],
+                left_sem.at[k],
+            ),
+        )
+
+    def remote(src, dst, send, recv, to_f, to_j):
+        return pltpu.make_async_remote_copy(
+            src_ref=src, dst_ref=dst, send_sem=send, recv_sem=recv,
+            device_id={"cd": to_f, "ij": to_j}, device_id_type=MESH,
+        )
+
+    def amp_copy(k, landing):
+        to_j = lax.rem(j + k, blocks)
+        slot = j if landing is None else to_j
+        columns = pl.ds(pl.multiple_of(to_j * dpiece, dpiece), dpiece)
+        return remote(
+            amp_ref.at[:, :, columns], amp_in.at[slot],
+            amp_send.at[to_j], amp_recv.at[slot], f, to_j,
+        )
+
+    def pair_copy(b):
+        return remote(
+            sums.at[b, 1 - core], pair_in.at[b], pair_send.at[b], pair_recv.at[b],
+            f + 1 - 2 * core, j,
+        )
+
+    def tile_copy(b, k, landing):
+        to_z = lax.rem(z + k, chips)
+        slot = z if landing is None else to_z
+        return remote(
+            joined.at[b, to_z], tiles_in.at[b, slot],
+            tile_send.at[b, to_z], tile_recv.at[b, slot], to_z * 2 + core, j,
+        )
+
+    def row_copy(k, landing):
+        flat = lax.rem(me + k, devices)
+        slot = me if landing is None else flat
+        return remote(
+            rows_out.at[flat], rows_in.at[slot], row_send.at[flat], row_recv.at[slot],
+            lax.rem(flat, formers), lax.div(flat, formers),
+        )
+
+    for k in range(depth_chunks):
+        for copy in load(k):
+            copy.start()
+
+    barrier = pltpu.get_barrier_semaphore()
+
+    @pl.loop(1, devices)
+    def _(k):
+        flat = lax.rem(me + k, devices)
+        pl.semaphore_signal(
+            barrier, inc=1,
+            device_id={"cd": lax.rem(flat, formers), "ij": lax.div(flat, formers)},
+            device_id_type=MESH,
+        )
+
+    to = lax.broadcasted_iota(jnp.int32, (SIDE, SIDE), 0)
+    origin = lax.broadcasted_iota(jnp.int32, (SIDE, SIDE), 1)
+    reorder = (origin == (to % per) * group + to // per).astype(jnp.bfloat16)
+    chosen = (
+        lax.broadcasted_iota(jnp.int32, (formers * tile, rows), 0) == label_ref[...]
+    ).astype(jnp.bfloat16)
+
+    for k in range(depth_chunks):
+        for copy in load(k):
+            copy.wait()
+
+        @pl.loop(0, kc // (2 * per))
+        def _(m):
+            base = pl.multiple_of(k * kc * group + m * (2 * SIDE), 2 * SIDE)
+            both = jnp.concatenate(
+                [right_v[pl.ds(base, SIDE), :], right_v[pl.ds(base + SIDE, SIDE), :]], axis=1
+            )
+            moved = jnp.dot(reorder, both, preferred_element_type=jnp.float32).astype(jnp.bfloat16)
+            first = pl.multiple_of(k * kc + m * (2 * per), 2 * per)
+            for g in range(group):
+                column = (g // nb) * LANES
+                piece = moved[g * per : (g + 1) * per]
+                stacked = jnp.concatenate([piece[:, :LANES], piece[:, LANES:]], axis=0)
+                sorted_v[g % nb, pl.ds(first, 2 * per), column : column + LANES] = stacked
+
+        product = jnp.dot(
+            left_v[:, k * kc : (k + 1) * kc],
+            sorted_v[0, k * kc : (k + 1) * kc, :],
+            preferred_element_type=jnp.float32,
+        )
+        if k == 0:
+            first_panel[...] = product
+            pl.semaphore_wait(barrier, devices - 1)
+            for n in range(1, blocks):
+                amp_copy(n, None).start()
+        else:
+            first_panel[...] = first_panel[...] + product
+
+    def add_rows(b, panel):
+        local = jnp.dot(chosen, panel.astype(jnp.bfloat16), preferred_element_type=jnp.float32)
+        sums[b] = local.reshape(2, chips, tile, dpiece)
+        pair_copy(b).start()
+
+    def join(b):
+        pair_copy(b).wait()
+        joined[b] = sums[b, core] + pair_in[b]
+        for n in range(1, chips):
+            tile_copy(b, n, None).start()
+        tiles_in[b, z] = joined[b, z]
+
+    add_rows(0, first_panel[...])
+
+    @pl.loop(1, nb)
+    def _(b):
+        panel = jnp.dot(left_v[...], sorted_v[b], preferred_element_type=jnp.float32)
+        join(b - 1)
+        add_rows(b, panel)
+
+    for n in range(1, blocks):
+        amp_copy(n, True).wait()
+    amp_in[j] = amp_ref[:, :, pl.ds(pl.multiple_of(j * dpiece, dpiece), dpiece)]
+    join(nb - 1)
+
+    def fold(x):
+        parts = [
+            x[r : r + 8, c : c + LANES]
+            for r in range(0, tile, 8)
+            for c in range(0, dpiece, LANES)
+        ]
+        return functools.reduce(jnp.add, parts)
+
+    for b in range(nb):
+        for n in range(1, chips):
+            tile_copy(b, n, True).wait()
+        whole = tiles_in[b, 0]
+        for n in range(1, chips):
+            whole = whole + tiles_in[b, n]
+        for s in range(blocks):
+            for i in range(ni):
+                rows_out[(s * ni + i) * nb + b] = jnp.sum(
+                    fold(amp_in[s, i] * whole), axis=0, keepdims=True
+                )
+
+    @pl.loop(1, devices)
+    def _(k):
+        row_copy(k, None).start()
+
+    rows_in[me] = rows_out[me]
+
+    @pl.loop(1, devices)
+    def _(k):
+        row_copy(k, True).wait()
+
+    total = rows_in[0]
+    for s in range(1, devices):
+        total = total + rows_in[s]
+    out_ref[...] = jnp.sum(total, axis=1, keepdims=True)
+
+
+def fits(left_factor, right_factor, amplitudes, formers, blocks):
+    depth, nb, dpiece = right_factor.shape
+    ni, tile, _ = amplitudes.shape
+    if dpiece % LANES or tile % 8 or left_factor.shape[0] % 16 or formers % 2:
+        return False
+    group = nb * (dpiece // LANES)
+    if SIDE % group or (SIDE // group) % 16 or nb < 2:
+        return False
+    if depth % (4 * SIDE) or ni * nb != formers:
+        return False
+    weights = 4 * depth * nb * dpiece + 2 * left_factor.size
+    held = 4 * formers * tile * nb * dpiece * 3
+    return held + weights < (40 << 20)
+
+
+def by_kernel(left_factor, right_factor, amplitudes, heights, owner_map, row_site):
+    formers = lax.axis_size("cd")
+    blocks = lax.axis_size("ij")
+    devices = formers * blocks
+    chips = formers // 2
+    rows, depth = left_factor.shape
+    _, nb, dpiece = right_factor.shape
+    ni, tile, _ = amplitudes.shape
+    lane_tiles = dpiece // LANES
+    chunks = 4
+    live = jnp.arange(rows, dtype=jnp.int32)[None, :] < heights[0]
+    owner = owner_map[:, :, 0]
+    label = jnp.where(live, ((owner % 2) * chips + owner // 2) * tile + row_site, -1)
+    flat_right = (
+        right_factor.reshape(depth, nb, lane_tiles, LANES)
+        .transpose(0, 2, 1, 3)
+        .reshape(depth * lane_tiles * nb, LANES)
+    )
+    vmem = pl.BlockSpec(memory_space=pltpu.VMEM)
+    hbm = pl.BlockSpec(memory_space=pl.ANY)
+    dma = pltpu.SemaphoreType.DMA
+    value = pl.pallas_call(
+        functools.partial(ladder_kernel, formers, blocks, nb, chunks),
+        out_shape=jax.ShapeDtypeStruct((1, 1), jnp.float32),
+        in_specs=[vmem, vmem, hbm, hbm],
+        out_specs=vmem,
+        scratch_shapes=[
+            pltpu.VMEM((rows, depth), jnp.bfloat16),
+            pltpu.VMEM((depth * lane_tiles * nb, LANES), jnp.bfloat16),
+            pltpu.VMEM((nb, depth, dpiece), jnp.bfloat16),
+            pltpu.VMEM((rows, dpiece), jnp.float32),
+            pltpu.VMEM((nb, 2, chips, tile, dpiece), jnp.float32),
+            pltpu.VMEM((nb, chips, tile, dpiece), jnp.float32),
+            pltpu.VMEM((nb, chips, tile, dpiece), jnp.float32),
+            pltpu.VMEM((nb, chips, tile, dpiece), jnp.float32),
+            pltpu.VMEM((blocks, ni, tile, dpiece), jnp.float32),
+            pltpu.VMEM((devices, 1, LANES), jnp.float32),
+            pltpu.VMEM((devices, 1, LANES), jnp.float32),
+            dma((chunks,)),
+            dma((chunks,)),
+            dma((blocks,)),
+            dma((blocks,)),
+            dma((nb,)),
+            dma((nb,)),
+            dma((nb, chips)),
+            dma((nb, chips)),
+            dma((devices,)),
+            dma((devices,)),
+        ],
+        compiler_params=pltpu.CompilerParams(
+            collective_id=0, has_side_effects=True, vmem_limit_bytes=56 << 20
+        ),
+    )(amplitudes, label, left_factor, flat_right)
+    return value.reshape(1)
 
 
 def contract(amplitudes, sums):
     return jnp.einsum("icd,cbd->ib", amplitudes, sums, precision=lax.Precision.HIGHEST)
 
 
-def on_device(left_factor, right_factor, amplitudes, heights, owner_map, row_site):
+def by_rows(left_factor, right_factor, amplitudes, heights, owner_map, row_site):
     rows = left_factor.shape[0]
     formers = lax.axis_size("cd")
     capacity = (rows + formers - 1) // formers + rows // (2 * formers)
@@ -55,6 +322,14 @@
     return lax.psum_scatter(partial_value.reshape(-1), "cd", scatter_dimension=0, tiled=True)
 
 
+def on_device(left_factor, right_factor, amplitudes, heights, owner_map, row_site):
+    args = (left_factor, right_factor, amplitudes, heights, owner_map, row_site)
+    sizes = lax.axis_size("cd"), lax.axis_size("ij")
+    if fits(left_factor, right_factor, amplitudes, *sizes):
+        return by_kernel(*args)
+    return by_rows(*args)
+
+
 def solution(mesh):
     placed = (
         P("cd", None),

time: 105 us -> 41.5 us (0.40)
  Pallas kernels: 0 us -> 38.2 us
  waiting for transfers between devices: 36.6 us -> 0 us
  blocking collectives: 23.1 us -> 0 us
  local copies, waits for them, and re-layouts: 15.5 us -> 0 us
  matrix products: 13.3 us -> 0 us
  starting transfers between devices: 11.4 us -> 0 us
  other arithmetic: 3.99 us -> 1.32 us
    pallas_call x0 -> x1, Pallas kernels: none -> 38.2 us  [by_kernel(): pl.pallas_call(functools.partial(ladder_kernel, formers, blocks, nb, chun...]
    all_to_all x2 -> x0, waiting for transfers between devices: 36.6 us -> none  [the longest x1 36.6 us: on_device(): lax.all_to_all(outgoing, 'cd', split_axis=0, concat_axis=0, tiled=True)]
    unnamed x1 -> x0, blocking collectives: 13.6 us -> none
    dot_general x4 -> x0, matrix products: 13.3 us -> none  [the longest x1 9.96 us: on_device(): jnp.dot(dispatch.astype(jnp.bfloat16), panel, preferred_element_type=jnp....]
    all_to_all x2 -> x0, starting transfers between devices: 11.4 us -> none  [the longest x1 6.33 us: on_device(): lax.all_to_all(labels, 'cd', split_axis=0, concat_axis=0, tiled=True)]
    unnamed x7 -> x0, local copies, waits for them, and re-layouts: 11.3 us -> none
    all_gather x1 -> x0, blocking collectives: 9.52 us -> none  [on_device(): lax.all_gather(jnp.einsum('cr,rbd->cbd', picker, arrived, preferred_eleme...]
    reshape x2 -> x0, local copies, waits for them, and re-layouts: 2.47 us -> none  [the longest x1 2.39 us: on_device(): outgoing = outgoing.reshape(formers, capacity, bwidth, dpiece)]
  transfers between devices with their start and end apart: 2 -> 0, of which waited for: 1 -> 0; matrix products, arithmetic and copies ran while one was open for 22% -> 0% of each run, Pallas kernels for 0% -> 0%
where the time goes in v1:
time: 41.5 us; the launch traced here: 41.3 us
  Pallas kernels  38.2 us (92%)
  between operations  1.72 us (4%)
  other arithmetic  1.32 us (3%)
    pallas_call x1, Pallas kernels, by_kernel(): pl.pallas_call(functools.partial(ladder_kernel, formers, blocks, nb, chun...  38.2 us
    select_n x1, other arithmetic, by_kernel(): jnp.where(live, (owner % 2 * chips + owner // 2) * tile + row_site, -1)  1.32 us

profile of v1, /device:TPU:0, one launch (start us, length us, event | category | flops | bytes accessed | tf_op | source)
XLA Modules:
  0.0 41.3 jit_solution(6309919984597333425)
XLA Ops:
  0.7 1.3 %compare_select_fusion.label_ref = s32[1,512]{1,0:T(1,128)} fusion(s32[1,512]{1,0:T(1,128)} %param.11, s32[1,512,1]{1,2,0:T(1,128)} %param.10, s32[]{:T(128)} %bitcast.22), kind=kLoop, calls=%fused_computation.2 | loop fusion | flops 12800 | bytes 6148 | tf_op jit(solution)/shard_map/jit(_where)/select_n | solution.py:230
  2.0 38.2 %shard_map.64 = f32[1,1]{1,0:T(1,128)} custom-call(f32[2,24,1024]{2,1,0:T(8,128)} %amp_ref.1, s32[1,512]{1,0:T(1,128)} %compare_select_fusion.label_ref, bf16[512,4096]{1,0:T(8,128)(2,1)} %left_ref.1, bf16[32768,128]{1,0:T(8,128)(2,1)} %bitcast.23), custom_call_target="tpu_custom_call" | custom-call | tf_op jit(solution)/shard_map/pallas_call | solution.py:239

commit v2 on v1

--- a/solution.py
+++ b/solution.py
@@ -14,7 +14,7 @@
 
 def ladder_kernel(
     formers, blocks, nb, depth_chunks,
-    amp_ref, label_ref, left_ref, right_ref, out_ref,
+    amp_ref, height_ref, owner_ref, site_ref, left_ref, right_ref, out_ref,
     left_v, right_v, sorted_v, first_panel, sums, pair_in, joined, tiles_in, amp_in, rows_out, rows_in,
     left_sem, right_sem, amp_send, amp_recv, pair_send, pair_recv,
     tile_send, tile_recv, row_send, row_recv,
@@ -32,6 +32,7 @@
     lane_tiles = right_v.shape[0] // (depth * nb)
     group = nb * lane_tiles
     per = SIDE // group
+    wide = 8
     dpiece = lane_tiles * LANES
     ni, tile, _ = amp_ref.shape
 
@@ -64,6 +65,10 @@
             amp_send.at[to_j], amp_recv.at[slot], f, to_j,
         )
 
+    def own_amp():
+        columns = pl.ds(pl.multiple_of(j * dpiece, dpiece), dpiece)
+        return pltpu.make_async_copy(amp_ref.at[:, :, columns], amp_in.at[j], amp_send.at[j])
+
     def pair_copy(b):
         return remote(
             sums.at[b, 1 - core], pair_in.at[b], pair_send.at[b], pair_recv.at[b],
@@ -78,13 +83,17 @@
             tile_send.at[b, to_z], tile_recv.at[b, slot], to_z * 2 + core, j,
         )
 
-    def row_copy(k, landing):
-        flat = lax.rem(me + k, devices)
-        slot = me if landing is None else flat
-        return remote(
-            rows_out.at[flat], rows_in.at[slot], row_send.at[flat], row_recv.at[slot],
-            lax.rem(flat, formers), lax.div(flat, formers),
-        )
+    def turned(at, step, size):
+        moved = at + step
+        return jnp.where(moved >= size, moved - size, moved)
+
+    near_f = [turned(f, n, formers) for n in range(formers)]
+    near_j = [turned(j, n, blocks) for n in range(blocks)]
+    others = [(pf, pj) for pj in near_j for pf in near_f][1:]
+
+    def row_copy(pf, pj):
+        flat = pj * formers + pf
+        return remote(rows_out.at[flat], rows_in.at[me], row_send, row_recv, pf, pj)
 
     for k in range(depth_chunks):
         for copy in load(k):
@@ -92,39 +101,44 @@
 
     barrier = pltpu.get_barrier_semaphore()
 
-    @pl.loop(1, devices)
-    def _(k):
-        flat = lax.rem(me + k, devices)
+    for pf, pj in others:
         pl.semaphore_signal(
-            barrier, inc=1,
-            device_id={"cd": lax.rem(flat, formers), "ij": lax.div(flat, formers)},
-            device_id_type=MESH,
+            barrier, inc=1, device_id={"cd": pf, "ij": pj}, device_id_type=MESH
         )
 
     to = lax.broadcasted_iota(jnp.int32, (SIDE, SIDE), 0)
     origin = lax.broadcasted_iota(jnp.int32, (SIDE, SIDE), 1)
     reorder = (origin == (to % per) * group + to // per).astype(jnp.bfloat16)
+    owner = owner_ref[...]
+    label = ((owner & 1) * chips + (owner >> 1)) * tile + site_ref[...]
+    live = lax.broadcasted_iota(jnp.int32, (1, rows), 1) < height_ref[...]
+    label = jnp.where(live, label, -1)
     chosen = (
-        lax.broadcasted_iota(jnp.int32, (formers * tile, rows), 0) == label_ref[...]
+        lax.broadcasted_iota(jnp.int32, (formers * tile, rows), 0) == label
     ).astype(jnp.bfloat16)
 
     for k in range(depth_chunks):
         for copy in load(k):
             copy.wait()
 
-        @pl.loop(0, kc // (2 * per))
+        span = per * wide
+
+        @pl.loop(0, kc // span, unroll=2)
         def _(m):
-            base = pl.multiple_of(k * kc * group + m * (2 * SIDE), 2 * SIDE)
-            both = jnp.concatenate(
-                [right_v[pl.ds(base, SIDE), :], right_v[pl.ds(base + SIDE, SIDE), :]], axis=1
-            )
-            moved = jnp.dot(reorder, both, preferred_element_type=jnp.float32).astype(jnp.bfloat16)
-            first = pl.multiple_of(k * kc + m * (2 * per), 2 * per)
+            base = pl.multiple_of(k * kc * group + m * (wide * SIDE), wide * SIDE)
+            pieces = [right_v[pl.ds(base + w * SIDE, SIDE), :] for w in range(wide)]
+            moved = jnp.dot(
+                reorder, jnp.concatenate(pieces, axis=1), preferred_element_type=jnp.float32
+            ).astype(jnp.bfloat16)
+            first = pl.multiple_of(k * kc + m * span, span)
             for g in range(group):
-                column = (g // nb) * LANES
+                b, part = g % nb, g // nb
+                column = (b % 2) * dpiece + part * LANES
                 piece = moved[g * per : (g + 1) * per]
-                stacked = jnp.concatenate([piece[:, :LANES], piece[:, LANES:]], axis=0)
-                sorted_v[g % nb, pl.ds(first, 2 * per), column : column + LANES] = stacked
+                stacked = jnp.concatenate(
+                    [piece[:, w * LANES : (w + 1) * LANES] for w in range(wide)], axis=0
+                )
+                sorted_v[b // 2, pl.ds(first, span), column : column + LANES] = stacked
 
         product = jnp.dot(
             left_v[:, k * kc : (k + 1) * kc],
@@ -136,13 +150,16 @@
             pl.semaphore_wait(barrier, devices - 1)
             for n in range(1, blocks):
                 amp_copy(n, None).start()
+            own_amp().start()
         else:
             first_panel[...] = first_panel[...] + product
 
-    def add_rows(b, panel):
+    def add_rows(h, panel):
         local = jnp.dot(chosen, panel.astype(jnp.bfloat16), preferred_element_type=jnp.float32)
-        sums[b] = local.reshape(2, chips, tile, dpiece)
-        pair_copy(b).start()
+        for b in (2 * h, 2 * h + 1):
+            part = local[:, (b % 2) * dpiece : (b % 2 + 1) * dpiece]
+            sums[b] = part.reshape(2, chips, tile, dpiece)
+            pair_copy(b).start()
 
     def join(b):
         pair_copy(b).wait()
@@ -153,15 +170,21 @@
 
     add_rows(0, first_panel[...])
 
-    @pl.loop(1, nb)
-    def _(b):
-        panel = jnp.dot(left_v[...], sorted_v[b], preferred_element_type=jnp.float32)
-        join(b - 1)
-        add_rows(b, panel)
+    half = depth // 2
+    for h in range(1, nb // 2):
+        panel = jnp.dot(
+            left_v[:, :half], sorted_v[h, :half, :], preferred_element_type=jnp.float32
+        )
+        join(2 * h - 2)
+        join(2 * h - 1)
+        add_rows(h, panel + jnp.dot(
+            left_v[:, half:], sorted_v[h, half:, :], preferred_element_type=jnp.float32
+        ))
 
     for n in range(1, blocks):
         amp_copy(n, True).wait()
-    amp_in[j] = amp_ref[:, :, pl.ds(pl.multiple_of(j * dpiece, dpiece), dpiece)]
+    own_amp().wait()
+    join(nb - 2)
     join(nb - 1)
 
     def fold(x):
@@ -184,15 +207,12 @@
                     fold(amp_in[s, i] * whole), axis=0, keepdims=True
                 )
 
-    @pl.loop(1, devices)
-    def _(k):
-        row_copy(k, None).start()
-
+    for pf, pj in others:
+        row_copy(pf, pj).start()
     rows_in[me] = rows_out[me]
-
-    @pl.loop(1, devices)
-    def _(k):
-        row_copy(k, True).wait()
+    most = pl.ds(0, devices - 1)
+    pltpu.make_async_copy(rows_in.at[most], rows_in.at[most], row_recv).wait()
+    pltpu.make_async_copy(rows_out.at[most], rows_out.at[most], row_send).wait()
 
     total = rows_in[0]
     for s in range(1, devices):
@@ -206,9 +226,9 @@
     if dpiece % LANES or tile % 8 or left_factor.shape[0] % 16 or formers % 2:
         return False
     group = nb * (dpiece // LANES)
-    if SIDE % group or (SIDE // group) % 16 or nb < 2:
+    if SIDE % group or (SIDE // group) % 16 or nb % 2:
         return False
-    if depth % (4 * SIDE) or ni * nb != formers:
+    if depth % (4 * 8 * (SIDE // group)) or ni * nb != formers:
         return False
     weights = 4 * depth * nb * dpiece + 2 * left_factor.size
     held = 4 * formers * tile * nb * dpiece * 3
@@ -225,9 +245,6 @@
     ni, tile, _ = amplitudes.shape
     lane_tiles = dpiece // LANES
     chunks = 4
-    live = jnp.arange(rows, dtype=jnp.int32)[None, :] < heights[0]
-    owner = owner_map[:, :, 0]
-    label = jnp.where(live, ((owner % 2) * chips + owner // 2) * tile + row_site, -1)
     flat_right = (
         right_factor.reshape(depth, nb, lane_tiles, LANES)
         .transpose(0, 2, 1, 3)
@@ -239,13 +256,13 @@
     value = pl.pallas_call(
         functools.partial(ladder_kernel, formers, blocks, nb, chunks),
         out_shape=jax.ShapeDtypeStruct((1, 1), jnp.float32),
-        in_specs=[vmem, vmem, hbm, hbm],
+        in_specs=[hbm, vmem, vmem, vmem, hbm, hbm],
         out_specs=vmem,
         scratch_shapes=[
             pltpu.VMEM((rows, depth), jnp.bfloat16),
             pltpu.VMEM((depth * lane_tiles * nb, LANES), jnp.bfloat16),
-            pltpu.VMEM((nb, depth, dpiece), jnp.bfloat16),
-            pltpu.VMEM((rows, dpiece), jnp.float32),
+            pltpu.VMEM((nb // 2, depth, 2 * dpiece), jnp.bfloat16),
+            pltpu.VMEM((rows, 2 * dpiece), jnp.float32),
             pltpu.VMEM((nb, 2, chips, tile, dpiece), jnp.float32),
             pltpu.VMEM((nb, chips, tile, dpiece), jnp.float32),
             pltpu.VMEM((nb, chips, tile, dpiece), jnp.float32),
@@ -261,13 +278,13 @@
             dma((nb,)),
             dma((nb, chips)),
             dma((nb, chips)),
-            dma((devices,)),
-            dma((devices,)),
+            dma,
+            dma,
         ],
         compiler_params=pltpu.CompilerParams(
             collective_id=0, has_side_effects=True, vmem_limit_bytes=56 << 20
         ),
-    )(amplitudes, label, left_factor, flat_right)
+    )(amplitudes, heights.reshape(1, 1), owner_map.reshape(1, rows), row_site, left_factor, flat_right)
     return value.reshape(1)
 
 

time: 41.5 us -> 31.9 us (0.77)
  Pallas kernels: 38.2 us -> 29.9 us
  other arithmetic: 1.32 us -> 0 us
    pallas_call x1, Pallas kernels: 38.2 us -> 29.9 us  [by_kernel(): pl.pallas_call(functools.partial(ladder_kernel, formers, blocks, nb, chun...]
    select_n x1 -> x0, other arithmetic: 1.32 us -> none  [by_kernel(): jnp.where(live, (owner % 2 * chips + owner // 2) * tile + row_site, -1)]
where the time goes in v2:
time: 31.9 us; the launch traced here: 31.7 us
  Pallas kernels  29.9 us (94%)
  between operations  1.85 us (6%)
    pallas_call x1, Pallas kernels, by_kernel(): pl.pallas_call(functools.partial(ladder_kernel, formers, blocks, nb, chun...  29.9 us

profile of v2, /device:TPU:0, one launch (start us, length us, event | category | flops | bytes accessed | tf_op | source)
XLA Modules:
  0.0 31.7 jit_solution(15546964247104540352)
XLA Ops:
  0.7 29.9 %shard_map.64 = f32[1,1]{1,0:T(1,128)} custom-call(f32[2,24,1024]{2,1,0:T(8,128)} %amp_ref.1, s32[1,1]{1,0:T(1,128)} %bitcast.8.height_ref, s32[1,512]{1,0:T(1,128)} %bitcast.10, s32[1,512]{1,0:T(1,128)} %site_ref.1, bf16[512,4096]{1,0:T(8,128)(2,1)} %left_ref.1, bf16[32768,128]{1,0:T(8,128)(2,1)} %bitcast.9), custom_call_target="tpu_custom_call" | custom-call | tf_op jit(solution)/shard_map/pallas_call | solution.py:256

commit v3 on v1

--- a/solution.py
+++ b/solution.py
@@ -14,7 +14,7 @@
 
 def ladder_kernel(
     formers, blocks, nb, depth_chunks,
-    amp_ref, label_ref, left_ref, right_ref, out_ref,
+    amp_ref, height_ref, owner_ref, site_ref, left_ref, right_ref, out_ref,
     left_v, right_v, sorted_v, first_panel, sums, pair_in, joined, tiles_in, amp_in, rows_out, rows_in,
     left_sem, right_sem, amp_send, amp_recv, pair_send, pair_recv,
     tile_send, tile_recv, row_send, row_recv,
@@ -78,13 +78,17 @@
             tile_send.at[b, to_z], tile_recv.at[b, slot], to_z * 2 + core, j,
         )
 
-    def row_copy(k, landing):
-        flat = lax.rem(me + k, devices)
-        slot = me if landing is None else flat
-        return remote(
-            rows_out.at[flat], rows_in.at[slot], row_send.at[flat], row_recv.at[slot],
-            lax.rem(flat, formers), lax.div(flat, formers),
-        )
+    def turned(at, step, size):
+        moved = at + step
+        return jnp.where(moved >= size, moved - size, moved)
+
+    near_f = [turned(f, n, formers) for n in range(formers)]
+    near_j = [turned(j, n, blocks) for n in range(blocks)]
+    others = [(pf, pj) for pj in near_j for pf in near_f][1:]
+
+    def row_copy(pf, pj):
+        flat = pj * formers + pf
+        return remote(rows_out.at[flat], rows_in.at[me], row_send, row_recv, pf, pj)
 
     for k in range(depth_chunks):
         for copy in load(k):
@@ -92,27 +96,27 @@
 
     barrier = pltpu.get_barrier_semaphore()
 
-    @pl.loop(1, devices)
-    def _(k):
-        flat = lax.rem(me + k, devices)
+    for pf, pj in others:
         pl.semaphore_signal(
-            barrier, inc=1,
-            device_id={"cd": lax.rem(flat, formers), "ij": lax.div(flat, formers)},
-            device_id_type=MESH,
+            barrier, inc=1, device_id={"cd": pf, "ij": pj}, device_id_type=MESH
         )
 
     to = lax.broadcasted_iota(jnp.int32, (SIDE, SIDE), 0)
     origin = lax.broadcasted_iota(jnp.int32, (SIDE, SIDE), 1)
     reorder = (origin == (to % per) * group + to // per).astype(jnp.bfloat16)
+    owner = owner_ref[...]
+    label = ((owner & 1) * chips + (owner >> 1)) * tile + site_ref[...]
+    live = lax.broadcasted_iota(jnp.int32, (1, rows), 1) < height_ref[...]
+    label = jnp.where(live, label, -1)
     chosen = (
-        lax.broadcasted_iota(jnp.int32, (formers * tile, rows), 0) == label_ref[...]
+        lax.broadcasted_iota(jnp.int32, (formers * tile, rows), 0) == label
     ).astype(jnp.bfloat16)
 
     for k in range(depth_chunks):
         for copy in load(k):
             copy.wait()
 
-        @pl.loop(0, kc // (2 * per))
+        @pl.loop(0, kc // (2 * per), unroll=8)
         def _(m):
             base = pl.multiple_of(k * kc * group + m * (2 * SIDE), 2 * SIDE)
             both = jnp.concatenate(
@@ -184,15 +188,12 @@
                     fold(amp_in[s, i] * whole), axis=0, keepdims=True
                 )
 
-    @pl.loop(1, devices)
-    def _(k):
-        row_copy(k, None).start()
-
+    for pf, pj in others:
+        row_copy(pf, pj).start()
     rows_in[me] = rows_out[me]
-
-    @pl.loop(1, devices)
-    def _(k):
-        row_copy(k, True).wait()
+    most = pl.ds(0, devices - 1)
+    pltpu.make_async_copy(rows_in.at[most], rows_in.at[most], row_recv).wait()
+    pltpu.make_async_copy(rows_out.at[most], rows_out.at[most], row_send).wait()
 
     total = rows_in[0]
     for s in range(1, devices):
@@ -224,10 +225,7 @@
     _, nb, dpiece = right_factor.shape
     ni, tile, _ = amplitudes.shape
     lane_tiles = dpiece // LANES
-    chunks = 4
-    live = jnp.arange(rows, dtype=jnp.int32)[None, :] < heights[0]
-    owner = owner_map[:, :, 0]
-    label = jnp.where(live, ((owner % 2) * chips + owner // 2) * tile + row_site, -1)
+    chunks = 2
     flat_right = (
         right_factor.reshape(depth, nb, lane_tiles, LANES)
         .transpose(0, 2, 1, 3)
@@ -239,7 +237,7 @@
     value = pl.pallas_call(
         functools.partial(ladder_kernel, formers, blocks, nb, chunks),
         out_shape=jax.ShapeDtypeStruct((1, 1), jnp.float32),
-        in_specs=[vmem, vmem, hbm, hbm],
+        in_specs=[vmem, vmem, vmem, vmem, hbm, hbm],
         out_specs=vmem,
         scratch_shapes=[
             pltpu.VMEM((rows, depth), jnp.bfloat16),
@@ -261,13 +259,13 @@
             dma((nb,)),
             dma((nb, chips)),
             dma((nb, chips)),
-            dma((devices,)),
-            dma((devices,)),
+            dma,
+            dma,
         ],
         compiler_params=pltpu.CompilerParams(
             collective_id=0, has_side_effects=True, vmem_limit_bytes=56 << 20
         ),
-    )(amplitudes, label, left_factor, flat_right)
+    )(amplitudes, heights.reshape(1, 1), owner_map.reshape(1, rows), row_site, left_factor, flat_right)
     return value.reshape(1)
 
 

time: 41.5 us -> 31.9 us (0.77)
  Pallas kernels: 38.2 us -> 29.9 us
  other arithmetic: 1.32 us -> 0 us
    pallas_call x1, Pallas kernels: 38.2 us -> 29.9 us  [by_kernel(): pl.pallas_call(functools.partial(ladder_kernel, formers, blocks, nb, chun...]
    select_n x1 -> x0, other arithmetic: 1.32 us -> none  [by_kernel(): jnp.where(live, (owner % 2 * chips + owner // 2) * tile + row_site, -1)]
where the time goes in v3:
time: 31.9 us; the launch traced here: 31.8 us
  Pallas kernels  29.9 us (94%)
  between operations  1.85 us (6%)
    pallas_call x1, Pallas kernels, by_kernel(): pl.pallas_call(functools.partial(ladder_kernel, formers, blocks, nb, chun...  29.9 us

profile of v3, /device:TPU:0, one launch (start us, length us, event | category | flops | bytes accessed | tf_op | source)
XLA Modules:
  0.0 31.8 jit_solution(13500770395496975365)
XLA Ops:
  0.7 29.9 %shard_map.64 = f32[1,1]{1,0:T(1,128)} custom-call(f32[2,24,1024]{2,1,0:T(8,128)} %amp_ref.1, s32[1,1]{1,0:T(1,128)} %bitcast.8.height_ref, s32[1,512]{1,0:T(1,128)} %bitcast.10, s32[1,512]{1,0:T(1,128)} %site_ref.1, bf16[512,4096]{1,0:T(8,128)(2,1)} %left_ref.1, bf16[32768,128]{1,0:T(8,128)(2,1)} %bitcast.9), custom_call_target="tpu_custom_call" | custom-call | tf_op jit(solution)/shard_map/pallas_call | solution.py:237
